TPU v7x, 256 devices: a whole 4x4x8 slice. The times are simulated.
256 devices in a mesh: frame: 32 (over x, y, core), head: 8 (over z).
Axes of the slice: x: 4, y: 4, z: 8, core: 2. Of those that a mesh axis runs over, the one named last changes fastest.
Arguments:
- queries: bfloat16 [7168, 3072], P('frame', 'head'), may hold values from -24 to 24
- key_rows: bfloat16 [7168, 3072], P('frame', 'head'), may hold values from -24 to 24
- value_rows: bfloat16 [7168, 3072], P('frame', 'head'), may hold values from -5 to 5
- ref_keys: bfloat16 [32, 1024, 3072], P('frame', None, 'head'), may hold values from -5 to 5
- ref_values: bfloat16 [32, 1024, 3072], P('frame', None, 'head'), may hold values from -5 to 5
- key_lists: int32 [32, 8], P('frame'), may hold values from 0 to 31, as said below
- list_counts: int32 [32], P('frame'), may hold values from 1 to 8, as said below
- owner_index: int32 [1], replicated, may hold values from 0 to 31
- out_weight: bfloat16 [3072, 3072], P('head'), may hold values from -1.5 to 1.5
- residual: bfloat16 [7168, 3072], P('frame', 'head'), may hold values from -3 to 3
- gate_scale: float32 [3072], P('head'), may hold values from 0.5 to 2
Outputs:
- block_out: bfloat16 [7168, 3072], P('frame', 'head')
Inputs may be any that keep to these rules, and one draw needn't show every extreme that they name: `key_lists`: the first list_counts[f] entries of row f are distinct frames other than f, each within 4 frames of f; the remaining entries equal f. `list_counts`: some frame lists every frame within 4 of it.
All inputs are finite; a program needn't handle non-finite values.
Results may differ from a plain program's by a relative error of at most 0.02.
Values may be sent and summed in bfloat16 or wider, within the bound.
A program may use at most 64 MiB of HBM per device.

v0:
```python
import math
import jax
import jax.numpy as jnp
from jax import lax
from jax.sharding import PartitionSpec as P

HD = 128
REACH = 4


def broadcast(block, axis, source):
    block = jnp.where(lax.axis_index(axis) == source, block, jnp.zeros_like(block))
    return lax.psum(block, axis)


def from_behind(block, axis, distance):
    devices = range(lax.axis_size(axis))
    route = [(i - distance, i) for i in devices if i - distance in devices]
    return lax.ppermute(block, axis, route)


def absorb(carried, query_heads, key_block, value_block, allowed):
    running_max, running_sum, weighted = carried
    head_count = query_heads.shape[1]
    key_heads = key_block.reshape(key_block.shape[0], head_count, HD)
    value_heads = value_block.reshape(value_block.shape[0], head_count, HD)
    scores = jnp.einsum(
        "qhd,khd->hqk", query_heads, key_heads, preferred_element_type=jnp.float32
    ) * (1.0 / math.sqrt(HD))
    if allowed is not None:
        scores = jnp.where(allowed[None, None, :], scores, -jnp.inf)
    new_max = jnp.maximum(running_max, jnp.max(scores, axis=-1))
    factor = jnp.exp(running_max - new_max)
    weights = jnp.exp(scores - new_max[:, :, None])
    running_sum = running_sum * factor + jnp.sum(weights, axis=-1)
    weighted = weighted * factor.T[:, :, None] + jnp.einsum(
        "hqk,khd->qhd",
        weights.astype(jnp.bfloat16),
        value_heads,
        preferred_element_type=jnp.float32,
    )
    return (new_max, running_sum, weighted)


def frame_block(carried, query_heads, key_block, value_block, begin_row, listed, live_slots):
    frame_of = (begin_row + jnp.arange(key_block.shape[0], dtype=jnp.int32)) // query_heads.shape[0]
    allowed = jnp.any((frame_of[:, None] == listed[None, :]) & live_slots[None, :], axis=1)
    return lax.cond(
        jnp.any(allowed),
        lambda current: absorb(current, query_heads, key_block, value_block, allowed),
        lambda current: current,
        carried,
    )


def per_device(
    queries,
    key_rows,
    value_rows,
    ref_keys,
    ref_values,
    key_lists,
    list_counts,
    owner_index,
    out_weight,
    residual,
    gate_scale,
):
    frame_len = queries.shape[0]
    columns_here = queries.shape[1]
    head_count = columns_here // HD
    query_heads = queries.reshape(frame_len, head_count, HD)
    listed = key_lists[0]
    live_slots = jnp.arange(listed.shape[0], dtype=jnp.int32) < list_counts[0]
    position = lax.axis_index("frame")
    carried = (
        jnp.full((head_count, frame_len), -jnp.inf, jnp.float32),
        jnp.zeros((head_count, frame_len), jnp.float32),
        jnp.zeros((frame_len, head_count, HD), jnp.float32),
    )
    style_keys, style_values = (
        broadcast(ref_keys, "frame", owner_index[0]),
        broadcast(ref_values, "frame", owner_index[0]),
    )
    carried = absorb(carried, query_heads, style_keys[0], style_values[0], None)
    carried = absorb(carried, query_heads, key_rows, value_rows, None)
    for offset in list(range(1, REACH + 1)) + list(range(-REACH, 0)):
        moved_keys, moved_values = from_behind((key_rows, value_rows), "frame", offset)
        carried = frame_block(
            carried,
            query_heads,
            moved_keys,
            moved_values,
            (position - offset) * frame_len,
            listed,
            live_slots,
        )
    running_max, running_sum, weighted = carried
    attended = (
        (weighted / running_sum.T[:, :, None]).astype(jnp.bfloat16).reshape(frame_len, columns_here)
    )
    shares = lax.psum_scatter(
        lax.dot_general(
            out_weight, attended, (((0,), (1,)), ((), ())), preferred_element_type=jnp.float32
        ).astype(jnp.bfloat16),
        "head",
        scatter_dimension=0,
        tiled=True,
    ).astype(jnp.float32)
    return (residual.astype(jnp.float32) + gate_scale[None, :] * shares.T).astype(jnp.bfloat16)


def solution(mesh):
    placed = (
        P("frame", "head"),
        P("frame", "head"),
        P("frame", "head"),
        P("frame", None, "head"),
        P("frame", None, "head"),
        P("frame", None),
        P("frame"),
        P(),
        P("head", None),
        P("frame", "head"),
        P("head"),
    )
    return jax.shard_map(
        per_device, mesh=mesh, in_specs=placed, out_specs=P("frame", "head"), check_vma=False
    )
```

profile of v0, /device:TPU:2, one launch (start us, length us, event | category | flops | bytes accessed | tf_op | source)
XLA Modules:
  0.0 269.7 jit_solution(7305506349866342035)
XLA Ops:
  6.5 1.9 copy.128
  8.4 1.9 collective-permute-start
  10.3 3.5 %collective-permute-start.2 = (bf16[224,384]{0,1:T(8,128)(2,1)}, bf16[224,384]{0,1:T(8,128)(2,1)}, u32[]{:S(2)}, u32[]{:S(2)}) collective-permute-start(bf16[224,384]{0,1:T(8,128)(2,1)} %copy.128), channel_id=1, source_target_pairs={{0,16},{8,24},{16,32},{24,40},{32,48},{40,56},{48,64},{56,72},{64,... | collective-permute-start | bytes 516104 | tf_op jit(solution)/shard_map/ppermute | solution.py:19
  13.8 1.1 copy.133
  14.9 3.3 %collective-permute-start.1 = (bf16[224,384]{0,1:T(8,128)(2,1)S(1)}, bf16[224,384]{0,1:T(8,128)(2,1)}, u32[]{:S(2)}, u32[]{:S(2)}) collective-permute-start(bf16[224,384]{0,1:T(8,128)(2,1)S(1)} %copy.133), channel_id=1, source_target_pairs={{0,8},{8,16},{16,24},{24,32},{32,40},{40,48},{48,56},{56,64},{64,7... | collective-permute-start | bytes 516104 | tf_op jit(solution)/shard_map/ppermute | solution.py:19
  18.2 3.2 %collective-permute-start.3 = (bf16[224,384]{0,1:T(8,128)(2,1)S(1)}, bf16[224,384]{0,1:T(8,128)(2,1)}, u32[]{:S(2)}, u32[]{:S(2)}) collective-permute-start(bf16[224,384]{0,1:T(8,128)(2,1)S(1)} %copy.133), channel_id=1, source_target_pairs={{0,16},{8,24},{16,32},{24,40},{32,48},{40,56},{48,64},{56,72},{64,... | collective-permute-start | bytes 516104 | tf_op jit(solution)/shard_map/ppermute | solution.py:19
  21.4 2.7 collective-permute-start.4
  24.7 2.3 copy.124
  27.0 1.2 copy.131
  29.2 2.3 copy.125
  31.5 1.2 copy.132
  34.6 1.5 fusion.89
  41.0 2.1 fusion.105
  43.1 108.5 %all-reduce.3.cloned.1.call-done = (bf16[1024,3,128]{2,0,1:T(8,128)(2,1)}, bf16[1024,3,128]{2,0,1:T(8,128)(2,1)}) async-done(((bf16[1024,3,128]{2,0,1:T(8,128)(2,1)}, bf16[1024,3,128]{2,0,1:T(8,128)(2,1)}), (bf16[1024,3,128]{2,0,1:T(8,128)(2,1)}, bf16[1024,3,128]{2,0,1:T(8,128)(2,1)})) %all-reduce.3.cloned.1.call-update) | async-done | bytes 1572880 | tf_op jit(solution)/shard_map/psum | solution.py:13
  151.6 1.9 bitcast_reduce_fusion
  154.5 1.9 collective-permute-start.5
  156.8 5.5 %collective-permute-start.6 = (bf16[224,384]{0,1:T(8,128)(2,1)}, bf16[224,384]{0,1:T(8,128)(2,1)S(1)}, u32[]{:S(2)}, u32[]{:S(2)}) collective-permute-start(bf16[224,384]{0,1:T(8,128)(2,1)} %copy.128), channel_id=1, source_target_pairs={{0,32},{8,40},{16,48},{24,56},{32,64},{40,72},{48,80},{56,88},{64,... | collective-permute-start | bytes 516104 | tf_op jit(solution)/shard_map/ppermute | solution.py:19
  162.3 2.8 %collective-permute-start.7 = (bf16[224,384]{0,1:T(8,128)(2,1)S(1)}, bf16[224,384]{0,1:T(8,128)(2,1)S(1)}, u32[]{:S(2)}, u32[]{:S(2)}) collective-permute-start(bf16[224,384]{0,1:T(8,128)(2,1)S(1)} %copy.133), channel_id=1, source_target_pairs={{0,32},{8,40},{16,48},{24,56},{32,64},{40,72},{48,80},{56,88},{64,... | collective-permute-start | bytes 516104 | tf_op jit(solution)/shard_map/ppermute | solution.py:19
  165.1 5.5 %collective-permute-start.8 = (bf16[224,384]{0,1:T(8,128)(2,1)}, bf16[224,384]{0,1:T(8,128)(2,1)S(1)}, u32[]{:S(2)}, u32[]{:S(2)}) collective-permute-start(bf16[224,384]{0,1:T(8,128)(2,1)} %copy.128), channel_id=1, source_target_pairs={{32,0},{40,8},{48,16},{56,24},{64,32},{72,40},{80,48},{88,56},{96,... | collective-permute-start | bytes 516104 | tf_op jit(solution)/shard_map/ppermute | solution.py:19
  170.6 1.9 collective-permute-start.9
  173.2 3.1 %collective-permute-start.10 = (bf16[224,384]{0,1:T(8,128)(2,1)}, bf16[224,384]{0,1:T(8,128)(2,1)S(1)}, u32[]{:S(2)}, u32[]{:S(2)}) collective-permute-start(bf16[224,384]{0,1:T(8,128)(2,1)} %copy.128), channel_id=1, source_target_pairs={{24,0},{32,8},{40,16},{48,24},{56,32},{64,40},{72,48},{80,56},{88,... | collective-permute-start | bytes 516104 | tf_op jit(solution)/shard_map/ppermute | solution.py:19
  177.1 1.9 collective-permute-start.11
  179.1 1.9 collective-permute-start.12
  181.0 1.9 collective-permute-start.13
  183.0 2.9 %collective-permute-start.14 = (bf16[224,384]{0,1:T(8,128)(2,1)}, bf16[224,384]{0,1:T(8,128)(2,1)}, u32[]{:S(2)}, u32[]{:S(2)}) collective-permute-start(bf16[224,384]{0,1:T(8,128)(2,1)} %copy.128), channel_id=1, source_target_pairs={{8,0},{16,8},{24,16},{32,24},{40,32},{48,40},{56,48},{64,56},{72,6... | collective-permute-start | bytes 516104 | tf_op jit(solution)/shard_map/ppermute | solution.py:19
  185.9 3.1 %collective-permute-done.10 = bf16[224,384]{0,1:T(8,128)(2,1)S(1)} collective-permute-done((bf16[224,384]{0,1:T(8,128)(2,1)}, bf16[224,384]{0,1:T(8,128)(2,1)S(1)}, u32[]{:S(2)}, u32[]{:S(2)}) %collective-permute-start.10) | collective-permute-done | bytes 172064 | tf_op jit(solution)/shard_map/ppermute | solution.py:19
  189.0 1.9 collective-permute-start.15
  191.0 2.8 %conditional.8 = ((f32[3,224]{1,0:T(4,128)S(1)}, f32[3,224]{1,0:T(4,128)S(1)}, f32[224,3,128]{2,0,1:T(8,128)S(1)})) conditional(s32[]{:T(128)} %convert_element_type.80, (f32[3,224]{1,0:T(4,128)S(1)}, f32[3,224]{1,0:T(4,128)S(1)}, f32[224,3,128]{2,0,1:T(8,128)S(1)}) %tuple.55, (pred[224]{0:T(512)(128)(4,1)S(1)}, bf16[224,384]{0,1:T(8,128)(2,1)}, ...), branch_computations={%region_15.16_spmd, %region_16.19_spmd} | conditional | flops 78298080 | bytes 3053824 | solution.py:48
  191.0 1.2 fusion.97
  192.4 1.4 fusion.1
  193.8 2.8 %conditional.10 = ((f32[3,224]{1,0:T(4,128)S(1)}, f32[3,224]{1,0:T(4,128)S(1)}, f32[224,3,128]{2,0,1:T(8,128)S(1)})) conditional(s32[]{:T(128)} %convert_element_type.78, (f32[3,224]{1,0:T(4,128)S(1)}, f32[3,224]{1,0:T(4,128)S(1)}, f32[224,3,128]{2,0,1:T(8,128)S(1)}) %get-tuple-element.510, (pred[224]{0:T(512)(128)(4,1)S(1)}, ...), branch_computations={%region_25.26_spmd, %region_26.29_spmd} | conditional | flops 78298080 | bytes 3053824 | solution.py:48
  193.8 1.2 fusion.99
  195.2 1.4 fusion.15
  196.6 2.8 %conditional.12 = ((f32[3,224]{1,0:T(4,128)S(1)}, f32[3,224]{1,0:T(4,128)S(1)}, f32[224,3,128]{2,0,1:T(8,128)S(1)})) conditional(s32[]{:T(128)} %convert_element_type.76, (f32[3,224]{1,0:T(4,128)S(1)}, f32[3,224]{1,0:T(4,128)S(1)}, f32[224,3,128]{2,0,1:T(8,128)S(1)}) %get-tuple-element.512, (pred[224]{0:T(512)(128)(4,1)S(1)}, ...), branch_computations={%region_35.36_spmd, %region_36.39_spmd} | conditional | flops 78298080 | bytes 3053824 | solution.py:48
  196.7 1.2 fusion.101
  198.1 1.4 fusion.29
  199.4 2.8 %conditional.13 = ((f32[3,224]{1,0:T(4,128)S(1)}, f32[3,224]{1,0:T(4,128)S(1)}, f32[224,3,128]{2,0,1:T(8,128)S(1)})) conditional(s32[]{:T(128)} %convert_element_type.75, (f32[3,224]{1,0:T(4,128)S(1)}, f32[3,224]{1,0:T(4,128)S(1)}, f32[224,3,128]{2,0,1:T(8,128)S(1)}) %get-tuple-element.513, (pred[224]{0:T(512)(128)(4,1)S(1)}, ...), branch_computations={%region_40.41_spmd, %region_41.44_spmd} | conditional | flops 78298080 | bytes 3053824 | solution.py:48
  199.5 1.2 fusion.102
  200.9 1.4 fusion.36
  202.3 2.8 %conditional.14 = ((f32[3,224]{1,0:T(4,128)S(1)}, f32[3,224]{1,0:T(4,128)S(1)}, f32[224,3,128]{2,0,1:T(8,128)S(1)})) conditional(s32[]{:T(128)} %convert_element_type.74, (f32[3,224]{1,0:T(4,128)S(1)}, f32[3,224]{1,0:T(4,128)S(1)}, f32[224,3,128]{2,0,1:T(8,128)S(1)}) %get-tuple-element.514, (pred[224,8]{0,1:T(8,128)(4,1)S(1)}, ...), branch_computations={%region_44.45_spmd, %region_45.49_spmd} | conditional | flops 78299648 | bytes 3055841 | solution.py:48
  202.3 1.2 fusion.103
  203.7 1.4 fusion.43
  205.1 1.9 conditional.15
  205.2 1.2 fusion.104
  207.3 2.0 fusion.56
  209.3 2.6 copy.198
  212.0 49.1 %reduce-scatter.4.cloned.1.call-done = bf16[384,224]{1,0:T(8,128)(2,1)} async-done(((bf16[3072,224]{1,0:T(8,128)(2,1)}), bf16[384,224]{1,0:T(8,128)(2,1)}) %reduce-scatter.4.cloned.1.call-update) | async-done | bytes 172048
  261.1 1.1 copy.199
  (92 shorter events, 7.5 us)
Async XLA Ops:
  6.5 200.8 %copy-start = (bf16[384,3072]{1,0:T(8,128)(2,1)S(1)}, bf16[384,3072]{1,0:T(8,128)(2,1)}, u32[]{:S(2)}) copy-start(bf16[384,3072]{1,0:T(8,128)(2,1)} %param.35) | copy-start | bytes 7077892
  6.5 20.5 %copy-start.2 = (bf16[1,1024,384]{2,1,0:T(8,128)(2,1)S(1)}, bf16[1,1024,384]{2,1,0:T(8,128)(2,1)}, u32[]{:S(2)}) copy-start(bf16[1,1024,384]{2,1,0:T(8,128)(2,1)} %param.31) | copy-start | bytes 2359300
  6.5 145.0 %all-reduce.3.cloned.1.call-start = ((), (), s32[]{:S(2)}) async-start(), calls=%async_computation.2 | async-start | bytes 3145728 | tf_op jit(solution)/shard_map/psum | solution.py:13
  8.4 146.1 %collective-permute-start = (bf16[224,384]{0,1:T(8,128)(2,1)}, bf16[224,384]{0,1:T(8,128)(2,1)}, u32[]{:S(2)}, u32[]{:S(2)}) collective-permute-start(bf16[224,384]{0,1:T(8,128)(2,1)} %copy.128), channel_id=1, source_target_pairs={{0,8},{8,16},{16,24},{24,32},{32,40},{40,48},{48,56},{56,64},{64,7... | collective-permute-start | bytes 516104 | tf_op jit(solution)/shard_map/ppermute | solution.py:19
  10.3 151.9 %collective-permute-start.2 = (bf16[224,384]{0,1:T(8,128)(2,1)}, bf16[224,384]{0,1:T(8,128)(2,1)}, u32[]{:S(2)}, u32[]{:S(2)}) collective-permute-start(bf16[224,384]{0,1:T(8,128)(2,1)} %copy.128), channel_id=1, source_target_pairs={{0,16},{8,24},{16,32},{24,40},{32,48},{40,56},{48,64},{56,72},{64,... | collective-permute-start | bytes 516104 | tf_op jit(solution)/shard_map/ppermute | solution.py:19
  14.9 141.9 %collective-permute-start.1 = (bf16[224,384]{0,1:T(8,128)(2,1)S(1)}, bf16[224,384]{0,1:T(8,128)(2,1)}, u32[]{:S(2)}, u32[]{:S(2)}) collective-permute-start(bf16[224,384]{0,1:T(8,128)(2,1)S(1)} %copy.133), channel_id=1, source_target_pairs={{0,8},{8,16},{16,24},{24,32},{32,40},{40,48},{48,56},{56,64},{64,7... | collective-permute-start | bytes 516104 | tf_op jit(solution)/shard_map/ppermute | solution.py:19
  18.2 146.9 %collective-permute-start.3 = (bf16[224,384]{0,1:T(8,128)(2,1)S(1)}, bf16[224,384]{0,1:T(8,128)(2,1)}, u32[]{:S(2)}, u32[]{:S(2)}) collective-permute-start(bf16[224,384]{0,1:T(8,128)(2,1)S(1)} %copy.133), channel_id=1, source_target_pairs={{0,16},{8,24},{16,32},{24,40},{32,48},{40,56},{48,64},{56,72},{64,... | collective-permute-start | bytes 516104 | tf_op jit(solution)/shard_map/ppermute | solution.py:19
  21.4 149.2 %collective-permute-start.4 = (bf16[224,384]{0,1:T(8,128)(2,1)}, bf16[224,384]{0,1:T(8,128)(2,1)}, u32[]{:S(2)}, u32[]{:S(2)}) collective-permute-start(bf16[224,384]{0,1:T(8,128)(2,1)} %copy.128), channel_id=1, source_target_pairs={{0,24},{8,32},{16,40},{24,48},{32,56},{40,64},{48,72},{56,80},{64,... | collective-permute-start | bytes 516104 | tf_op jit(solution)/shard_map/ppermute | solution.py:19
  32.7 228.4 %reduce-scatter.4.cloned.1.call-start = ((), (), s32[]{:S(2)}) async-start(), calls=%async_computation.1 | async-start | bytes 1769472
  151.6 1.9 copy-start.13
  153.4 3.0 %copy-start.1 = (f32[3,224,224]{1,2,0:T(8,128)S(1)}, f32[3,224,224]{1,2,0:T(8,128)}, u32[]{:S(2)}) copy-start(f32[3,224,224]{1,2,0:T(8,128)} %get-tuple-element.450) | copy-start | bytes 1806340
  154.5 36.5 %copy-start.12 = (pred[224]{0:T(512)(128)(4,1)S(1)}, pred[224]{0:T(512)(128)(4,1)}, u32[]{:S(2)}) copy-start(pred[224]{0:T(512)(128)(4,1)} %get-tuple-element.394) | copy-start | bytes 676
  154.5 18.1 %collective-permute-start.5 = (bf16[224,384]{0,1:T(8,128)(2,1)S(1)}, bf16[224,384]{0,1:T(8,128)(2,1)S(1)}, u32[]{:S(2)}, u32[]{:S(2)}) collective-permute-start(bf16[224,384]{0,1:T(8,128)(2,1)S(1)} %copy.133), channel_id=1, source_target_pairs={{0,24},{8,32},{16,40},{24,48},{32,56},{40,64},{48,72},{56,80},{64,... | collective-permute-start | bytes 516104 | tf_op jit(solution)/shard_map/ppermute | solution.py:19
  156.8 20.3 %collective-permute-start.6 = (bf16[224,384]{0,1:T(8,128)(2,1)}, bf16[224,384]{0,1:T(8,128)(2,1)S(1)}, u32[]{:S(2)}, u32[]{:S(2)}) collective-permute-start(bf16[224,384]{0,1:T(8,128)(2,1)} %copy.128), channel_id=1, source_target_pairs={{0,32},{8,40},{16,48},{24,56},{32,64},{40,72},{48,80},{56,88},{64,... | collective-permute-start | bytes 516104 | tf_op jit(solution)/shard_map/ppermute | solution.py:19
  162.3 16.8 %collective-permute-start.7 = (bf16[224,384]{0,1:T(8,128)(2,1)S(1)}, bf16[224,384]{0,1:T(8,128)(2,1)S(1)}, u32[]{:S(2)}, u32[]{:S(2)}) collective-permute-start(bf16[224,384]{0,1:T(8,128)(2,1)S(1)} %copy.133), channel_id=1, source_target_pairs={{0,32},{8,40},{16,48},{24,56},{32,64},{40,72},{48,80},{56,88},{64,... | collective-permute-start | bytes 516104 | tf_op jit(solution)/shard_map/ppermute | solution.py:19
  165.1 15.9 %collective-permute-start.8 = (bf16[224,384]{0,1:T(8,128)(2,1)}, bf16[224,384]{0,1:T(8,128)(2,1)S(1)}, u32[]{:S(2)}, u32[]{:S(2)}) collective-permute-start(bf16[224,384]{0,1:T(8,128)(2,1)} %copy.128), channel_id=1, source_target_pairs={{32,0},{40,8},{48,16},{56,24},{64,32},{72,40},{80,48},{88,56},{96,... | collective-permute-start | bytes 516104 | tf_op jit(solution)/shard_map/ppermute | solution.py:19
  170.6 12.3 %collective-permute-start.9 = (bf16[224,384]{0,1:T(8,128)(2,1)S(1)}, bf16[224,384]{0,1:T(8,128)(2,1)S(1)}, u32[]{:S(2)}, u32[]{:S(2)}) collective-permute-start(bf16[224,384]{0,1:T(8,128)(2,1)S(1)} %copy.133), channel_id=1, source_target_pairs={{32,0},{40,8},{48,16},{56,24},{64,32},{72,40},{80,48},{88,56},{96,... | collective-permute-start | bytes 516104 | tf_op jit(solution)/shard_map/ppermute | solution.py:19
  172.5 0.7 copy-start.5
  173.2 15.8 %collective-permute-start.10 = (bf16[224,384]{0,1:T(8,128)(2,1)}, bf16[224,384]{0,1:T(8,128)(2,1)S(1)}, u32[]{:S(2)}, u32[]{:S(2)}) collective-permute-start(bf16[224,384]{0,1:T(8,128)(2,1)} %copy.128), channel_id=1, source_target_pairs={{24,0},{32,8},{40,16},{48,24},{56,32},{64,40},{72,48},{80,56},{88,... | collective-permute-start | bytes 516104 | tf_op jit(solution)/shard_map/ppermute | solution.py:19
  177.0 16.8 %copy-start.11 = (pred[224]{0:T(512)(128)(4,1)S(1)}, pred[224]{0:T(512)(128)(4,1)}, u32[]{:S(2)}) copy-start(pred[224]{0:T(512)(128)(4,1)} %get-tuple-element.396) | copy-start | bytes 676
  177.1 13.9 %copy-start.8 = (bf16[224,384]{0,1:T(8,128)(2,1)}, bf16[224,384]{0,1:T(8,128)(2,1)S(1)}, u32[]{:S(2)}) copy-start(bf16[224,384]{0,1:T(8,128)(2,1)S(1)} %collective-permute-done.6) | copy-start | bytes 516100
  177.1 22.3 %collective-permute-start.11 = (bf16[224,384]{0,1:T(8,128)(2,1)S(1)}, bf16[224,384]{0,1:T(8,128)(2,1)}, u32[]{:S(2)}, u32[]{:S(2)}) collective-permute-start(bf16[224,384]{0,1:T(8,128)(2,1)S(1)} %copy.133), channel_id=1, source_target_pairs={{24,0},{32,8},{40,16},{48,24},{56,32},{64,40},{72,48},{80,56},{88,... | collective-permute-start | bytes 516104 | tf_op jit(solution)/shard_map/ppermute | solution.py:19
  179.1 6.8 %copy-start.4 = (bf16[224,384]{0,1:T(8,128)(2,1)}, bf16[224,384]{0,1:T(8,128)(2,1)S(1)}, u32[]{:S(2)}) copy-start(bf16[224,384]{0,1:T(8,128)(2,1)S(1)} %collective-permute-done.7) | copy-start | bytes 516100
  179.1 23.2 %collective-permute-start.12 = (bf16[224,384]{0,1:T(8,128)(2,1)}, bf16[224,384]{0,1:T(8,128)(2,1)}, u32[]{:S(2)}, u32[]{:S(2)}) collective-permute-start(bf16[224,384]{0,1:T(8,128)(2,1)} %copy.128), channel_id=1, source_target_pairs={{16,0},{24,8},{32,16},{40,24},{48,32},{56,40},{64,48},{72,56},{80,... | collective-permute-start | bytes 516104 | tf_op jit(solution)/shard_map/ppermute | solution.py:19
  181.0 10.0 %copy-start.7 = (bf16[224,384]{0,1:T(8,128)(2,1)}, bf16[224,384]{0,1:T(8,128)(2,1)S(1)}, u32[]{:S(2)}) copy-start(bf16[224,384]{0,1:T(8,128)(2,1)S(1)} %collective-permute-done.8) | copy-start | bytes 516100
  181.0 21.2 %collective-permute-start.13 = (bf16[224,384]{0,1:T(8,128)(2,1)S(1)}, bf16[224,384]{0,1:T(8,128)(2,1)}, u32[]{:S(2)}, u32[]{:S(2)}) collective-permute-start(bf16[224,384]{0,1:T(8,128)(2,1)S(1)} %copy.133), channel_id=1, source_target_pairs={{16,0},{24,8},{32,16},{40,24},{48,32},{56,40},{64,48},{72,56},{80,... | collective-permute-start | bytes 516104 | tf_op jit(solution)/shard_map/ppermute | solution.py:19
  183.0 2.9 %copy-start.3 = (bf16[224,384]{0,1:T(8,128)(2,1)}, bf16[224,384]{0,1:T(8,128)(2,1)S(1)}, u32[]{:S(2)}) copy-start(bf16[224,384]{0,1:T(8,128)(2,1)S(1)} %collective-permute-done.9) | copy-start | bytes 516100
  183.0 22.1 %collective-permute-start.14 = (bf16[224,384]{0,1:T(8,128)(2,1)}, bf16[224,384]{0,1:T(8,128)(2,1)}, u32[]{:S(2)}, u32[]{:S(2)}) collective-permute-start(bf16[224,384]{0,1:T(8,128)(2,1)} %copy.128), channel_id=1, source_target_pairs={{8,0},{16,8},{24,16},{32,24},{40,32},{48,40},{56,48},{64,56},{72,6... | collective-permute-start | bytes 516104 | tf_op jit(solution)/shard_map/ppermute | solution.py:19
  189.0 1.9 copy-start.6
  189.0 16.1 %collective-permute-start.15 = (bf16[224,384]{0,1:T(8,128)(2,1)S(1)}, bf16[224,384]{0,1:T(8,128)(2,1)S(1)}, u32[]{:S(2)}, u32[]{:S(2)}) collective-permute-start(bf16[224,384]{0,1:T(8,128)(2,1)S(1)} %copy.133), channel_id=1, source_target_pairs={{8,0},{16,8},{24,16},{32,24},{40,32},{48,40},{56,48},{64,56},{72,6... | collective-permute-start | bytes 516104 | tf_op jit(solution)/shard_map/ppermute | solution.py:19
  209.3 52.8 %copy-start.9 = (bf16[224,384]{1,0:T(8,128)(2,1)S(1)}, bf16[224,384]{1,0:T(8,128)(2,1)}, u32[]{:S(2)}) copy-start(bf16[224,384]{1,0:T(8,128)(2,1)} %param.36) | copy-start | bytes 516100
  209.3 52.8 %copy-start.10 = (f32[384]{0:T(512)S(1)}, f32[384]{0:T(512)}, u32[]{:S(2)}) copy-start(f32[384]{0:T(512)} %param.37) | copy-start | bytes 4612
Sparse Core Ops, SparseCore 0:
  32.8 118.6 all-reduce.2
  212.1 48.9 reduce-scatter.3
where the time goes:
time: 271 us; the launch traced here: 270 us
  waiting for transfers between devices  161 us (59%)
  starting transfers between devices  45.9 us (17%)
  matrix products  21.9 us (8%)
  between operations  20.2 us (7%)
  local copies, waits for them, and re-layouts  15.5 us (6%)
  other arithmetic  5.24 us (2%)
    psum x1, waiting for transfers between devices, broadcast(): return lax.psum(block, axis)  109 us
    unnamed x3, waiting for transfers between devices  49.2 us
    ppermute x16, starting transfers between devices, from_behind(): return lax.ppermute(block, axis, route)  45.8 us
    unnamed x35, local copies, waits for them, and re-layouts  11.9 us
    dot_general x8, matrix products, absorb(): jnp.einsum('qhd,khd->hqk', query_heads, key_heads, preferred_element_type...  11.4 us
    dot_general x8, matrix products, absorb(): jnp.einsum('hqk,khd->qhd', weights.astype(jnp.bfloat16), value_heads, pre...  8.54 us
  transfers between devices with their start and end apart: 18, of which 3 were waited for; matrix products, arithmetic and copies ran while one was open for 12% of the time, Pallas kernels for 0%

commit v1 on v0

--- a/solution.py
+++ b/solution.py
@@ -10,7 +10,7 @@
 
 def broadcast(block, axis, source):
     block = jnp.where(lax.axis_index(axis) == source, block, jnp.zeros_like(block))
-    return lax.psum(block, axis)
+    return jnp.sum(lax.all_gather(block, axis), axis=0)
 
 
 def from_behind(block, axis, distance):

time: 271 us -> 354 us (1.31)
  waiting for transfers between devices: 161 us -> 210 us
  other arithmetic: 5.24 us -> 33.2 us
  starting transfers between devices: 45.9 us -> 54.8 us
  local copies, waits for them, and re-layouts: 15.5 us -> 9.94 us
    all_gather x0 -> x2, waiting for transfers between devices: none -> 161 us  [broadcast(): return jnp.sum(lax.all_gather(block, axis), axis=0)]
    psum x1 -> x0, waiting for transfers between devices: 109 us -> none  [broadcast(): return lax.psum(block, axis)]
    reduce_sum x0 -> x2, other arithmetic: none -> 27.6 us  [broadcast(): return jnp.sum(lax.all_gather(block, axis), axis=0)]
    ppermute x16, starting transfers between devices: 45.8 us -> 54.7 us  [from_behind(): return lax.ppermute(block, axis, route)]
    unnamed x35 -> x37, local copies, waits for them, and re-layouts: 11.9 us -> 5.13 us
    reduce_sum x0 -> x2, local copies, waits for them, and re-layouts: none -> 4.65 us  [broadcast(): return jnp.sum(lax.all_gather(block, axis), axis=0)]
    unnamed x3 -> x4, waiting for transfers between devices: 49.2 us -> 49 us
  transfers between devices with their start and end apart: 18 -> 19, of which waited for: 3 -> 3; matrix products, arithmetic and copies ran while one was open for 12% -> 16% of each run, Pallas kernels for 0% -> 0%
where the time goes in v1:
time: 354 us; the launch traced here: 353 us
  waiting for transfers between devices  210 us (59%)
  starting transfers between devices  54.8 us (15%)
  other arithmetic  33.2 us (9%)
  matrix products  24.5 us (7%)
  between operations  20.3 us (6%)
  local copies, waits for them, and re-layouts  9.94 us (3%)
    all_gather x2, waiting for transfers between devices, broadcast(): return jnp.sum(lax.all_gather(block, axis), axis=0)  161 us
    ppermute x16, starting transfers between devices, from_behind(): return lax.ppermute(block, axis, route)  54.7 us
    unnamed x4, waiting for transfers between devices  49 us
    reduce_sum x2, other arithmetic, broadcast(): return jnp.sum(lax.all_gather(block, axis), axis=0)  27.6 us
    dot_general x8, matrix products, absorb(): jnp.einsum('qhd,khd->hqk', query_heads, key_heads, preferred_element_type...  12 us
    dot_general x8, matrix products, absorb(): jnp.einsum('hqk,khd->qhd', weights.astype(jnp.bfloat16), value_heads, pre...  10.5 us
  transfers between devices with their start and end apart: 19, of which 3 were waited for; matrix products, arithmetic and copies ran while one was open for 16% of the time, Pallas kernels for 0%

profile of v1, /device:TPU:2, one launch (start us, length us, event | category | flops | bytes accessed | tf_op | source)
XLA Modules:
  0.0 353.1 jit_solution(2810025348053548197)
XLA Ops:
  7.4 1.0 broadcast_select_fusion.1
  9.7 1.9 collective-permute-start
  11.6 3.5 collective-permute-start.2
  15.2 3.3 collective-permute-start.1
  18.5 3.2 collective-permute-start.3
  21.7 5.0 %collective-permute-start.4 = (bf16[224,384]{0,1:T(8,128)(2,1)S(1)}, bf16[224,384]{0,1:T(8,128)(2,1)}, u32[]{:S(2)}, u32[]{:S(2)}) collective-permute-start(bf16[224,384]{0,1:T(8,128)(2,1)S(1)} %copy.126), channel_id=1, source_target_pairs={{0,24},{8,32},{16,40},{24,48},{32,56},{40,64},{48,72},{56,80},{64,... | collective-permute-start | bytes 516104 | tf_op jit(solution)/shard_map/ppermute | solution.py:19
  26.8 1.1 copy.123
  34.6 1.2 fusion.105
  35.8 81.3 %all-gather.5.cloned.1.call-done = bf16[32,1024,384]{2,1,0:T(8,128)(2,1)} async-done(((bf16[1,1024,384]{2,1,0:T(8,128)(2,1)}), bf16[32,1024,384]{2,1,0:T(8,128)(2,1)}) %all-gather.5.cloned.1.call-update) | async-done | bytes 25165840 | tf_op jit(solution)/shard_map/all_gather | solution.py:13
  117.1 13.8 %reduce.12 = bf16[1024,384]{1,0:T(8,128)(2,1)} reduce(bf16[32,1024,384]{2,1,0:T(8,128)(2,1)} %all-gather.5.cloned.1.call-done, bf16[]{:T(256)} %constant.122.clone.1), dimensions={0}, to_apply=%region_8.9 | reduce | flops 12189696 | bytes 25952258 | tf_op jit(solution)/shard_map/reduce_sum | solution.py:13
  130.9 2.4 copy.122
  133.3 3.4 bitcast_reduce_fusion
  136.7 79.6 %all-gather.7.cloned.1.call-done = bf16[32,1024,384]{2,1,0:T(8,128)(2,1)} async-done(((bf16[1,1024,384]{2,1,0:T(8,128)(2,1)}), bf16[32,1024,384]{2,1,0:T(8,128)(2,1)}) %all-gather.7.cloned.1.call-update) | async-done | bytes 25165840 | tf_op jit(solution)/shard_map/all_gather | solution.py:13
  216.3 13.8 %reduce.13 = bf16[1024,384]{1,0:T(8,128)(2,1)} reduce(bf16[32,1024,384]{2,1,0:T(8,128)(2,1)} %all-gather.7.cloned.1.call-done, bf16[]{:T(256)} %constant.122.clone.1), dimensions={0}, to_apply=%region_13.14 | reduce | flops 12189696 | bytes 25952258 | tf_op jit(solution)/shard_map/reduce_sum | solution.py:13
  230.1 2.3 copy.129
  232.4 2.9 fusion.71
  235.3 1.9 collective-permute-start.5
  237.6 4.1 %collective-permute-start.6 = (bf16[224,384]{0,1:T(8,128)(2,1)S(1)}, bf16[224,384]{0,1:T(8,128)(2,1)S(1)}, u32[]{:S(2)}, u32[]{:S(2)}) collective-permute-start(bf16[224,384]{0,1:T(8,128)(2,1)S(1)} %copy.126), channel_id=1, source_target_pairs={{0,32},{8,40},{16,48},{24,56},{32,64},{40,72},{48,80},{56,88},{64,... | collective-permute-start | bytes 516104 | tf_op jit(solution)/shard_map/ppermute | solution.py:19
  241.7 4.2 %collective-permute-start.7 = (bf16[224,384]{0,1:T(8,128)(2,1)S(1)}, bf16[224,384]{0,1:T(8,128)(2,1)S(1)}, u32[]{:S(2)}, u32[]{:S(2)}) collective-permute-start(bf16[224,384]{0,1:T(8,128)(2,1)S(1)} %copy.131), channel_id=1, source_target_pairs={{0,32},{8,40},{16,48},{24,56},{32,64},{40,72},{48,80},{56,88},{64,... | collective-permute-start | bytes 516104 | tf_op jit(solution)/shard_map/ppermute | solution.py:19
  245.9 4.0 %collective-permute-start.8 = (bf16[224,384]{0,1:T(8,128)(2,1)S(1)}, bf16[224,384]{0,1:T(8,128)(2,1)S(1)}, u32[]{:S(2)}, u32[]{:S(2)}) collective-permute-start(bf16[224,384]{0,1:T(8,128)(2,1)S(1)} %copy.126), channel_id=1, source_target_pairs={{32,0},{40,8},{48,16},{56,24},{64,32},{72,40},{80,48},{88,56},{96,... | collective-permute-start | bytes 516104 | tf_op jit(solution)/shard_map/ppermute | solution.py:19
  250.0 3.3 collective-permute-start.9
  253.3 2.0 collective-permute-start.10
  256.1 1.9 collective-permute-start.11
  258.1 2.3 collective-permute-start.12
  260.4 10.1 %collective-permute-start.13 = (bf16[224,384]{0,1:T(8,128)(2,1)S(1)}, bf16[224,384]{0,1:T(8,128)(2,1)}, u32[]{:S(2)}, u32[]{:S(2)}) collective-permute-start(bf16[224,384]{0,1:T(8,128)(2,1)S(1)} %copy.131), channel_id=1, source_target_pairs={{16,0},{24,8},{32,16},{40,24},{48,32},{56,40},{64,48},{72,56},{80,... | collective-permute-start | bytes 516104 | tf_op jit(solution)/shard_map/ppermute | solution.py:19
  270.5 1.9 collective-permute-start.14
  272.5 2.0 collective-permute-start.15
  274.6 2.8 conditional.8
  274.6 1.2 fusion.97
  276.0 1.4 fusion.1
  277.4 2.8 conditional.10
  277.5 1.2 fusion.99
  278.9 1.4 fusion.15
  280.3 2.8 conditional.12
  280.3 1.2 fusion.101
  281.7 1.4 fusion.29
  283.1 2.8 conditional.13
  283.1 1.2 fusion.102
  284.5 1.4 fusion.36
  285.9 3.0 conditional.14
  286.1 1.2 fusion.103
  287.5 1.4 fusion.43
  288.9 1.9 conditional.15
  289.0 1.2 fusion.104
  291.1 2.0 fusion.56
  293.1 2.6 copy.198
  295.8 49.0 %reduce-scatter.4.cloned.1.call-done = bf16[384,224]{1,0:T(8,128)(2,1)} async-done(((bf16[3072,224]{1,0:T(8,128)(2,1)}), bf16[384,224]{1,0:T(8,128)(2,1)}) %reduce-scatter.4.cloned.1.call-update) | async-done | bytes 172048
  344.8 1.1 copy.199
  (100 shorter events, 6.1 us)
Async XLA Ops:
  6.5 284.6 %copy-start = (bf16[384,3072]{1,0:T(8,128)(2,1)S(1)}, bf16[384,3072]{1,0:T(8,128)(2,1)}, u32[]{:S(2)}) copy-start(bf16[384,3072]{1,0:T(8,128)(2,1)} %param.35) | copy-start | bytes 7077892
  6.5 3.0 copy-start.11
  6.5 8.5 %copy-start.12 = (bf16[224,384]{1,0:T(8,128)(2,1)S(1)}, bf16[224,384]{1,0:T(8,128)(2,1)}, u32[]{:S(2)}) copy-start(bf16[224,384]{1,0:T(8,128)(2,1)} %param.29) | copy-start | bytes 516100
  6.5 110.6 %all-gather.5.cloned.1.call-start = ((), (), s32[]{:S(2)}) async-start(), calls=%async_computation.1 | async-start | bytes 25952256 | tf_op jit(solution)/shard_map/all_gather | solution.py:13
  7.3 21.3 %copy-start.15 = (s32[1,8]{1,0:T(1,128)S(1)}, s32[1,8]{1,0:T(1,128)}, u32[]{:S(2)}) copy-start(s32[1,8]{1,0:T(1,128)} %param.32) | copy-start | bytes 100
  8.4 207.9 %all-gather.7.cloned.1.call-start = ((), (), s32[]{:S(2)}) async-start(), calls=%async_computation.2 | async-start | bytes 25952256 | tf_op jit(solution)/shard_map/all_gather | solution.py:13
  9.4 335.3 %reduce-scatter.4.cloned.1.call-start = ((), (), s32[]{:S(2)}) async-start(), calls=%async_computation.3 | async-start | bytes 1769472
  9.7 225.6 %collective-permute-start = (bf16[224,384]{0,1:T(8,128)(2,1)S(1)}, bf16[224,384]{0,1:T(8,128)(2,1)S(1)}, u32[]{:S(2)}, u32[]{:S(2)}) collective-permute-start(bf16[224,384]{0,1:T(8,128)(2,1)S(1)} %copy.126), channel_id=1, source_target_pairs={{0,8},{8,16},{16,24},{24,32},{32,40},{40,48},{48,56},{56,64},{64,7... | collective-permute-start | bytes 516104 | tf_op jit(solution)/shard_map/ppermute | solution.py:19
  11.6 230.1 %collective-permute-start.2 = (bf16[224,384]{0,1:T(8,128)(2,1)S(1)}, bf16[224,384]{0,1:T(8,128)(2,1)}, u32[]{:S(2)}, u32[]{:S(2)}) collective-permute-start(bf16[224,384]{0,1:T(8,128)(2,1)S(1)} %copy.126), channel_id=1, source_target_pairs={{0,16},{8,24},{16,32},{24,40},{32,48},{40,56},{48,64},{56,72},{64,... | collective-permute-start | bytes 516104 | tf_op jit(solution)/shard_map/ppermute | solution.py:19
  15.2 222.4 %collective-permute-start.1 = (bf16[224,384]{0,1:T(8,128)(2,1)S(1)}, bf16[224,384]{0,1:T(8,128)(2,1)}, u32[]{:S(2)}, u32[]{:S(2)}) collective-permute-start(bf16[224,384]{0,1:T(8,128)(2,1)S(1)} %copy.131), channel_id=1, source_target_pairs={{0,8},{8,16},{16,24},{24,32},{32,40},{40,48},{48,56},{56,64},{64,7... | collective-permute-start | bytes 516104 | tf_op jit(solution)/shard_map/ppermute | solution.py:19
  18.5 227.3 %collective-permute-start.3 = (bf16[224,384]{0,1:T(8,128)(2,1)S(1)}, bf16[224,384]{0,1:T(8,128)(2,1)S(1)}, u32[]{:S(2)}, u32[]{:S(2)}) collective-permute-start(bf16[224,384]{0,1:T(8,128)(2,1)S(1)} %copy.131), channel_id=1, source_target_pairs={{0,16},{8,24},{16,32},{24,40},{32,48},{40,56},{48,64},{56,72},{64,... | collective-permute-start | bytes 516104 | tf_op jit(solution)/shard_map/ppermute | solution.py:19
  21.7 228.2 %collective-permute-start.4 = (bf16[224,384]{0,1:T(8,128)(2,1)S(1)}, bf16[224,384]{0,1:T(8,128)(2,1)}, u32[]{:S(2)}, u32[]{:S(2)}) collective-permute-start(bf16[224,384]{0,1:T(8,128)(2,1)S(1)} %copy.126), channel_id=1, source_target_pairs={{0,24},{8,32},{16,40},{24,48},{32,56},{40,64},{48,72},{56,80},{64,... | collective-permute-start | bytes 516104 | tf_op jit(solution)/shard_map/ppermute | solution.py:19
  232.4 4.9 %copy-start.2 = (f32[3,224,224]{1,2,0:T(8,128)S(1)}, f32[3,224,224]{1,2,0:T(8,128)}, u32[]{:S(2)}) copy-start(f32[3,224,224]{1,2,0:T(8,128)} %get-tuple-element.448) | copy-start | bytes 1806340
  232.4 22.9 %copy-start.1 = (f32[3,1024,224]{1,2,0:T(8,128)S(1)}, f32[3,1024,224]{1,2,0:T(8,128)}, u32[]{:S(2)}) copy-start(f32[3,1024,224]{1,2,0:T(8,128)} %get-tuple-element.446) | copy-start | bytes 8257540
  235.3 1.9 copy-start.8
  235.3 18.0 %collective-permute-start.5 = (bf16[224,384]{0,1:T(8,128)(2,1)S(1)}, bf16[224,384]{0,1:T(8,128)(2,1)S(1)}, u32[]{:S(2)}, u32[]{:S(2)}) collective-permute-start(bf16[224,384]{0,1:T(8,128)(2,1)S(1)} %copy.131), channel_id=1, source_target_pairs={{0,24},{8,32},{16,40},{24,48},{32,56},{40,64},{48,72},{56,80},{64,... | collective-permute-start | bytes 516104 | tf_op jit(solution)/shard_map/ppermute | solution.py:19
  237.6 18.5 %collective-permute-start.6 = (bf16[224,384]{0,1:T(8,128)(2,1)S(1)}, bf16[224,384]{0,1:T(8,128)(2,1)S(1)}, u32[]{:S(2)}, u32[]{:S(2)}) collective-permute-start(bf16[224,384]{0,1:T(8,128)(2,1)S(1)} %copy.126), channel_id=1, source_target_pairs={{0,32},{8,40},{16,48},{24,56},{32,64},{40,72},{48,80},{56,88},{64,... | collective-permute-start | bytes 516104 | tf_op jit(solution)/shard_map/ppermute | solution.py:19
  241.7 16.4 %collective-permute-start.7 = (bf16[224,384]{0,1:T(8,128)(2,1)S(1)}, bf16[224,384]{0,1:T(8,128)(2,1)S(1)}, u32[]{:S(2)}, u32[]{:S(2)}) collective-permute-start(bf16[224,384]{0,1:T(8,128)(2,1)S(1)} %copy.131), channel_id=1, source_target_pairs={{0,32},{8,40},{16,48},{24,56},{32,64},{40,72},{48,80},{56,88},{64,... | collective-permute-start | bytes 516104 | tf_op jit(solution)/shard_map/ppermute | solution.py:19
  245.9 26.6 %copy-start.3 = (bf16[224,384]{0,1:T(8,128)(2,1)}, bf16[224,384]{0,1:T(8,128)(2,1)S(1)}, u32[]{:S(2)}) copy-start(bf16[224,384]{0,1:T(8,128)(2,1)S(1)} %collective-permute-done.3) | copy-start | bytes 516100
  245.9 14.5 %collective-permute-start.8 = (bf16[224,384]{0,1:T(8,128)(2,1)S(1)}, bf16[224,384]{0,1:T(8,128)(2,1)S(1)}, u32[]{:S(2)}, u32[]{:S(2)}) collective-permute-start(bf16[224,384]{0,1:T(8,128)(2,1)S(1)} %copy.126), channel_id=1, source_target_pairs={{32,0},{40,8},{48,16},{56,24},{64,32},{72,40},{80,48},{88,56},{96,... | collective-permute-start | bytes 516104 | tf_op jit(solution)/shard_map/ppermute | solution.py:19
  250.0 20.6 %collective-permute-start.9 = (bf16[224,384]{0,1:T(8,128)(2,1)S(1)}, bf16[224,384]{0,1:T(8,128)(2,1)S(1)}, u32[]{:S(2)}, u32[]{:S(2)}) collective-permute-start(bf16[224,384]{0,1:T(8,128)(2,1)S(1)} %copy.131), channel_id=1, source_target_pairs={{32,0},{40,8},{48,16},{56,24},{64,32},{72,40},{80,48},{88,56},{96,... | collective-permute-start | bytes 516104 | tf_op jit(solution)/shard_map/ppermute | solution.py:19
  253.3 21.3 %copy-start.6 = (bf16[224,384]{0,1:T(8,128)(2,1)}, bf16[224,384]{0,1:T(8,128)(2,1)S(1)}, u32[]{:S(2)}) copy-start(bf16[224,384]{0,1:T(8,128)(2,1)S(1)} %collective-permute-done.5) | copy-start | bytes 516100
  253.3 19.2 %collective-permute-start.10 = (bf16[224,384]{0,1:T(8,128)(2,1)S(1)}, bf16[224,384]{0,1:T(8,128)(2,1)S(1)}, u32[]{:S(2)}, u32[]{:S(2)}) collective-permute-start(bf16[224,384]{0,1:T(8,128)(2,1)S(1)} %copy.126), channel_id=1, source_target_pairs={{24,0},{32,8},{40,16},{48,24},{56,32},{64,40},{72,48},{80,56},{88,... | collective-permute-start | bytes 516104 | tf_op jit(solution)/shard_map/ppermute | solution.py:19
  256.1 18.5 %copy-start.10 = (bf16[224,384]{0,1:T(8,128)(2,1)}, bf16[224,384]{0,1:T(8,128)(2,1)S(1)}, u32[]{:S(2)}) copy-start(bf16[224,384]{0,1:T(8,128)(2,1)S(1)} %collective-permute-done.6) | copy-start | bytes 516100
  256.1 26.9 %collective-permute-start.11 = (bf16[224,384]{0,1:T(8,128)(2,1)S(1)}, bf16[224,384]{0,1:T(8,128)(2,1)}, u32[]{:S(2)}, u32[]{:S(2)}) collective-permute-start(bf16[224,384]{0,1:T(8,128)(2,1)S(1)} %copy.131), channel_id=1, source_target_pairs={{24,0},{32,8},{40,16},{48,24},{56,32},{64,40},{72,48},{80,56},{88,... | collective-permute-start | bytes 516104 | tf_op jit(solution)/shard_map/ppermute | solution.py:19
  258.1 16.5 %copy-start.5 = (bf16[224,384]{0,1:T(8,128)(2,1)}, bf16[224,384]{0,1:T(8,128)(2,1)S(1)}, u32[]{:S(2)}) copy-start(bf16[224,384]{0,1:T(8,128)(2,1)S(1)} %collective-permute-done.7) | copy-start | bytes 516100
  258.1 27.8 %collective-permute-start.12 = (bf16[224,384]{0,1:T(8,128)(2,1)S(1)}, bf16[224,384]{0,1:T(8,128)(2,1)}, u32[]{:S(2)}, u32[]{:S(2)}) collective-permute-start(bf16[224,384]{0,1:T(8,128)(2,1)S(1)} %copy.126), channel_id=1, source_target_pairs={{16,0},{24,8},{32,16},{40,24},{48,32},{56,40},{64,48},{72,56},{80,... | collective-permute-start | bytes 516104 | tf_op jit(solution)/shard_map/ppermute | solution.py:19
  260.4 14.2 %copy-start.9 = (bf16[224,384]{0,1:T(8,128)(2,1)}, bf16[224,384]{0,1:T(8,128)(2,1)S(1)}, u32[]{:S(2)}) copy-start(bf16[224,384]{0,1:T(8,128)(2,1)S(1)} %collective-permute-done.8) | copy-start | bytes 516100
  260.4 25.5 %collective-permute-start.13 = (bf16[224,384]{0,1:T(8,128)(2,1)S(1)}, bf16[224,384]{0,1:T(8,128)(2,1)}, u32[]{:S(2)}, u32[]{:S(2)}) collective-permute-start(bf16[224,384]{0,1:T(8,128)(2,1)S(1)} %copy.131), channel_id=1, source_target_pairs={{16,0},{24,8},{32,16},{40,24},{48,32},{56,40},{64,48},{72,56},{80,... | collective-permute-start | bytes 516104 | tf_op jit(solution)/shard_map/ppermute | solution.py:19
  270.5 4.0 %copy-start.4 = (bf16[224,384]{0,1:T(8,128)(2,1)}, bf16[224,384]{0,1:T(8,128)(2,1)S(1)}, u32[]{:S(2)}) copy-start(bf16[224,384]{0,1:T(8,128)(2,1)S(1)} %collective-permute-done.9) | copy-start | bytes 516100
  270.5 18.4 %collective-permute-start.14 = (bf16[224,384]{0,1:T(8,128)(2,1)S(1)}, bf16[224,384]{0,1:T(8,128)(2,1)}, u32[]{:S(2)}, u32[]{:S(2)}) collective-permute-start(bf16[224,384]{0,1:T(8,128)(2,1)S(1)} %copy.126), channel_id=1, source_target_pairs={{8,0},{16,8},{24,16},{32,24},{40,32},{48,40},{56,48},{64,56},{72,6... | collective-permute-start | bytes 516104 | tf_op jit(solution)/shard_map/ppermute | solution.py:19
  272.5 2.1 copy-start.7
  272.5 16.4 %collective-permute-start.15 = (bf16[224,384]{0,1:T(8,128)(2,1)S(1)}, bf16[224,384]{0,1:T(8,128)(2,1)S(1)}, u32[]{:S(2)}, u32[]{:S(2)}) collective-permute-start(bf16[224,384]{0,1:T(8,128)(2,1)S(1)} %copy.131), channel_id=1, source_target_pairs={{8,0},{16,8},{24,16},{32,24},{40,32},{48,40},{56,48},{64,56},{72,6... | collective-permute-start | bytes 516104 | tf_op jit(solution)/shard_map/ppermute | solution.py:19
  293.1 52.7 %copy-start.13 = (bf16[224,384]{1,0:T(8,128)(2,1)S(1)}, bf16[224,384]{1,0:T(8,128)(2,1)}, u32[]{:S(2)}) copy-start(bf16[224,384]{1,0:T(8,128)(2,1)} %param.36) | copy-start | bytes 516100
  293.1 52.7 %copy-start.14 = (f32[384]{0:T(512)S(1)}, f32[384]{0:T(512)}, u32[]{:S(2)}) copy-start(f32[384]{0:T(512)} %param.37) | copy-start | bytes 4612
Sparse Core Ops, SparseCore 0:
  9.9 107.1 all-gather.4
  119.7 96.5 all-gather.6
  295.9 48.8 reduce-scatter.3
